TPU v7x, 512 devices: a whole 4x8x8 slice. The times are simulated.
512 devices in a mesh: row: 64 (over x, y, core), col: 8 (over z).
Axes of the slice: x: 4, y: 8, z: 8, core: 2. Of those that a mesh axis runs over, the one named last changes fastest.
Arguments:
- tile_values: bfloat16 [65536, 128, 128], P(('row', 'col')), may hold values from 0 to 4000, as said below
- tile_rows: int32 [65536], P(('row', 'col')), may hold values from 0 to 3, as said below
- tile_cols: int32 [65536], P(('row', 'col')), may hold values from 0 to 63
- tile_count: int32 [512], P(('row', 'col')), may hold values from 32 to 128, as said below
- sketch: bfloat16 [256, 65536], P('row', 'col'), may hold values from -0.0234375 to 0.0234375
Outputs:
- embed_rows: float32 [32768, 256], P(('row', 'col'))
- gram: float32 [256, 256], replicated
Inputs may be any that keep to these rules, and one draw needn't show every extreme that they name: `tile_rows`: within one device the used and unused slots name distinct tile positions. `tile_count`: some device uses all 128 slots. `tile_values`: Nonnegative.
All inputs are finite; a program needn't handle non-finite values.
Results may differ from a plain program's by a relative error of at most 0.0029.
Values may be sent and summed in bfloat16 or wider, within the bound.
A program may use at most 64 MiB of HBM per device.

v0:
```python
import jax
import jax.numpy as jnp
from jax import lax
from jax.sharding import PartitionSpec as P

RT = 4
CT = 64


def local(tile_values, tile_rows, tile_cols, tile_count, sketch):
    slots = tile_values.shape[0]
    edge = tile_values.shape[1]
    width = sketch.shape[0] * lax.axis_size("row")
    own_rows = RT * edge
    valid = (jnp.arange(slots, dtype=jnp.int32) < tile_count[0]).astype(jnp.float32)
    row_onehot = (tile_rows[:, None] == jnp.arange(RT, dtype=jnp.int32)[None, :]).astype(
        jnp.float32
    )
    col_onehot = (tile_cols[:, None] == jnp.arange(CT, dtype=jnp.int32)[None, :]).astype(
        jnp.float32
    )
    row_terms = jnp.sum(tile_values, axis=2, dtype=jnp.float32) * valid[:, None]
    col_terms = jnp.sum(tile_values, axis=1, dtype=jnp.float32) * valid[:, None]
    row_part = jnp.einsum(
        "tr,ti->ri", row_onehot, row_terms, precision=lax.Precision.HIGHEST
    ).reshape(own_rows)
    col_part = jnp.einsum(
        "tc,tj->cj", col_onehot, col_terms, precision=lax.Precision.HIGHEST
    ).reshape(CT * edge)
    local_total = jnp.sum(row_part)
    row_sum = lax.psum(row_part, "col")
    column_total_sum = lax.psum(col_part, "row")
    volume = lax.psum(local_total, ("row", "col"))
    row_deg = (1.0 + row_sum).reshape(RT, edge)
    col_deg = (1.0 + column_total_sum).reshape(CT, edge)
    gathered = lax.all_gather(sketch, "row", axis=0, tiled=True)
    sketch3 = gathered.reshape(width, CT, edge)
    block = 16
    nblocks = (tile_count[0] + block - 1) // block

    def step(index, acc):
        start = index * block
        values = lax.dynamic_slice_in_dim(tile_values, start, block, 0)
        rows = lax.dynamic_slice_in_dim(tile_rows, start, block, 0)
        cols = lax.dynamic_slice_in_dim(tile_cols, start, block, 0)
        usable = lax.dynamic_slice_in_dim(valid, start, block, 0)
        rdeg = jnp.take(row_deg, rows, axis=0)
        cdeg = jnp.take(col_deg, cols, axis=0)
        ratio = volume * values.astype(jnp.float32) / (rdeg[:, :, None] * cdeg[:, None, :])
        logm = (jnp.log(jnp.maximum(ratio, 1.0)) * usable[:, None, None]).astype(jnp.bfloat16)
        picked = jnp.take(sketch3, cols, axis=1)
        contrib = jnp.einsum("tij,ktj->tik", logm, picked, preferred_element_type=jnp.float32)
        onehot = (rows[:, None] == jnp.arange(RT, dtype=jnp.int32)[None, :]).astype(jnp.float32)
        return acc + jnp.einsum("tr,tik->rik", onehot, contrib, precision=lax.Precision.HIGHEST)

    start_acc = jnp.zeros((RT, edge, width), jnp.float32)
    partial_value = lax.fori_loop(0, nblocks, step, start_acc).reshape(own_rows, width)
    overall_row_count = own_rows * lax.axis_size("row")
    share = own_rows // lax.axis_size("col")
    summed = lax.psum(partial_value, "col")
    local_gram = jnp.dot(
        summed.T, summed, precision=lax.Precision.HIGHEST, preferred_element_type=jnp.float32
    )
    gram = lax.psum(local_gram, "row") / overall_row_count
    embed_rows = lax.dynamic_slice_in_dim(summed, lax.axis_index("col") * share, share, 0)
    return (embed_rows, gram)


def solution(mesh):
    placed = (
        P(("row", "col"), None, None),
        P(("row", "col")),
        P(("row", "col")),
        P(("row", "col")),
        P("row", "col"),
    )
    return jax.shard_map(
        local, mesh=mesh, in_specs=placed, out_specs=(P(("row", "col"), None), P()), check_vma=False
    )
```

profile of v0, /device:TPU:1, one launch (start us, length us, event | category | flops | bytes accessed | tf_op | source)
XLA Modules:
  0.0 719.5 jit_solution(10749091998201171229)
XLA Ops:
  7.2 0.0 copy-start
  7.2 0.0 copy-start.1
  7.2 0.0 all-gather.3.cloned.1.call-start
  7.2 0.7 all-gather.3.cloned.1.call-update
  7.9 0.0 all-reduce.3.cloned.1.call-start
  8.6 3.4 convert_reduce_fusion
  12.0 0.0 copy-done
  12.1 0.9 fusion.29
  12.9 106.9 %psum.35 = f32[]{:T(128)} all-reduce(f32[]{:T(128)} %get-tuple-element.113), channel_id=1, replica_groups=mesh['row'=64,'col'=8] {'row','col'}, use_global_device_ids=true, to_apply=%region_5.0 | all-reduce | flops 1 | bytes 8 | tf_op jit(solution)/shard_map/psum | solution.py:33
  119.8 11.9 %psum.36 = f32[512]{0:T(512)S(1)} all-reduce(f32[512]{0:T(512)S(1)} %bitcast.26), channel_id=1, replica_groups=mesh['row'=64,'col'=8] {'col'}, use_global_device_ids=true, to_apply=%region_1.0 | all-reduce | flops 512 | bytes 4096 | tf_op jit(solution)/shard_map/psum | solution.py:31
  131.8 0.0 copy-done.1
  131.8 0.3 convolution_bitcast_fusion
  132.1 245.0 %psum.37 = f32[8192]{0:T(1024)S(1)} all-reduce(f32[8192]{0:T(1024)S(1)} %convolution_bitcast_fusion), channel_id=1, replica_groups=mesh['row'=64,'col'=8] {'row'}, use_global_device_ids=true, to_apply=%region_3.0 | all-reduce | flops 8192 | bytes 65536 | tf_op jit(solution)/shard_map/psum | solution.py:32
  377.1 0.0 all-gather.3.cloned.1.call-done
  377.1 8.4 %reshape.75 = bf16[256,64,128]{2,1,0:T(8,128)(2,1)} reshape(bf16[64,4,8192]{2,1,0:T(4,128)(2,1)} %all-gather.3.cloned.1.call-done) | data formatting | bytes 8388608 | tf_op jit(solution)/shard_map/reshape | solution.py:37
  385.5 6.8 copy.13
  392.4 0.1 broadcast_in_dim.46
  392.4 27.7 %while.10 = (s32[]{:T(128)}, f32[4,128,256]{2,0,1:T(4,128)S(1)}, s32[]{:T(128)}, s32[128]{0:T(128)S(1)}, f32[]{:T(128)}, /*index=5*/bf16[128,128,128]{2,1,0:T(8,...) while((s32[]{:T(128)}, f32[4,128,256]{2,0,1:T(4,128)S(1)}, ...), condition=%wide.region_7.8_spmd, body=%wide.region_6.7_spmd.sunk | while | flops 161880368 | bytes 9004759 | solution.py:57
  392.5 0.1 dynamic_slice.27
  392.5 0.1 compare_and_fusion.3
  392.6 0.6 gather_fusion.2
  393.2 0.1 broadcast_select_fusion.5
  393.3 0.6 gather_fusion.1
  393.8 0.1 broadcast_select_fusion.4
  393.9 2.9 gather_fusion
  396.9 2.2 fusion.41
  399.1 2.6 fusion.42
  401.7 0.1 dynamic_slice.27
  401.8 0.1 compare_and_fusion.3
  401.9 0.6 gather_fusion.2
  402.4 0.1 broadcast_select_fusion.5
  402.5 0.6 gather_fusion.1
  403.1 0.1 broadcast_select_fusion.4
  403.1 2.9 gather_fusion
  406.1 2.2 fusion.41
  408.3 2.6 fusion.42
  410.9 0.1 dynamic_slice.27
  411.0 0.1 compare_and_fusion.3
  411.1 0.6 gather_fusion.2
  411.7 0.1 broadcast_select_fusion.5
  411.7 0.6 gather_fusion.1
  412.3 0.1 broadcast_select_fusion.4
  412.4 2.9 gather_fusion
  415.3 2.2 fusion.41
  417.5 2.6 fusion.42
  420.1 0.9 copy.14
  421.0 0.0 all-reduce.3.cloned.1.call-update
  421.0 0.0 all-reduce.5.cloned.1.call-start
  421.1 96.7 %all-reduce.3.cloned.1.call-done = f32[512,256]{1,0:T(8,128)} async-done(((f32[512,256]{1,0:T(8,128)}), f32[512,256]{1,0:T(8,128)}) %all-reduce.3.cloned.1.call-update) | async-done | bytes 524304 | tf_op jit(solution)/shard_map/psum | solution.py:60
  517.8 2.9 fusion.30
  520.7 0.0 all-reduce.5.cloned.1.call-update
  520.8 1.5 constant_dynamic-slice_fusion
  522.2 189.1 %all-reduce.5.cloned.1.call-done = f32[256,256]{1,0:T(8,128)} async-done(((f32[256,256]{1,0:T(8,128)}), f32[256,256]{1,0:T(8,128)}) %all-reduce.5.cloned.1.call-update) | async-done | bytes 262160 | tf_op jit(solution)/shard_map/psum | solution.py:64
  711.4 1.7 broadcast_multiply_fusion
  (12 shorter events, 0.1 us)
Async XLA Ops:
  7.2 4.9 copy-start
  7.2 124.6 %copy-start.1 = (s32[128]{0:T(128)S(1)}, s32[128]{0:T(128)}, u32[]{:S(2)}) copy-start(s32[128]{0:T(128)} %param.9) | copy-start | bytes 1540
  7.2 369.9 %all-gather.3.cloned.1.call-start = ((), (), s32[]{:S(2)}) async-start(), calls=%async_computation.2 | async-start | bytes 4259840 | tf_op jit(solution)/shard_map/all_gather | solution.py:36
  7.9 509.9 %all-reduce.3.cloned.1.call-start = ((), (), s32[]{:S(2)}) async-start(), calls=%async_computation | async-start | bytes 1048576 | tf_op jit(solution)/shard_map/psum | solution.py:60
  421.0 290.3 %all-reduce.5.cloned.1.call-start = ((), (), s32[]{:S(2)}) async-start(), calls=%async_computation.1 | async-start | bytes 524288 | tf_op jit(solution)/shard_map/psum | solution.py:64
Sparse Core Ops, SparseCore 0:
  11.4 90.2 all-gather.2
  421.2 96.6 all-reduce.2
  522.3 189.0 all-reduce.4
where the time goes:
time: 721 us; the launch traced here: 720 us
  blocking collectives  364 us (50%)
  waiting for transfers between devices  287 us (40%)
  local copies, waits for them, and re-layouts  30.1 us (4%)
  matrix products  18.5 us (3%)
  between operations  14.5 us (2%)
    psum x1, blocking collectives, local(): column_total_sum = lax.psum(col_part, 'row')  245 us
    psum x1, waiting for transfers between devices, local(): gram = lax.psum(local_gram, 'row') / overall_row_count  189 us
    psum x1, blocking collectives, local(): volume = lax.psum(local_total, ('row', 'col'))  107 us
    psum x1, waiting for transfers between devices, local(): summed = lax.psum(partial_value, 'col')  96.7 us
  transfers between devices with their start and end apart: 3, of which 2 were waited for; matrix products, arithmetic and copies ran while one was open for 1% of the time, Pallas kernels for 0%

commit v1 on v0

v1 whole, which is shorter than its diff:
```python
import jax
import jax.numpy as jnp
from jax import lax
from jax.experimental import pallas as pl
from jax.experimental.pallas import tpu as pltpu
from jax.sharding import PartitionSpec as P

MESH = pl.DeviceIdType.MESH
F32 = jnp.float32
BF16 = jnp.bfloat16

TS = 128
RT = 4
CT = 64
SLOTS = 128
K = 256
X, Y, Z = 4, 8, 8
U = 2 * X
ROW = X * Y * 2
NR = ROW * RT * TS
OWN = RT * TS
SHARE = OWN // Z
KROWS = 4
NT_DIMS = (((1,), (1,)), ((), ()))


def wrap(value, n):
    return lax.rem(value + 4 * n, n)


def each(n, f):
    def step(m, carry):
        f(m)
        return carry

    lax.fori_loop(1, n, step, 0)


def kernel(
    rows_v,
    cols_v,
    rows_s,
    cols_s,
    count_s,
    sketch,
    tiles,
    embed,
    gram,
    a,
    logm,
    gath,
    weights,
    acc,
    xf,
    inv_v,
    inv_s,
    colpart,
    colsrc,
    ycol,
    rowbuf,
    zrow,
    xdeg,
    ydeg,
    rscale,
    cinv,
    psend,
    precv,
    gsrc,
    gz,
    g64,
    gy,
    gx,
    gfull,
    gfin,
    tile_sem,
    inv_sem,
    ag_send,
    ag_recv,
    small_send,
    small_recv,
):
    row = lax.axis_index("row")
    z = lax.axis_index("col")
    core = lax.rem(row, 2)
    y = lax.rem(row // 2, Y)
    x = row // (2 * Y)
    u = 2 * x + core

    def y_peer(m):
        return wrap(y + m, Y)

    def u_peer(m):
        return wrap(u + m, U)

    def z_peer(m):
        return wrap(z + m, Z)

    def y_device(v):
        return ((x * Y + v) * 2 + core, z)

    def u_device(v):
        return ((v // 2 * Y + y) * 2 + lax.rem(v, 2), z)

    def z_device(v):
        return (row, v)

    part = SLOTS // 4
    tile_copies = [
        pltpu.make_async_copy(
            tiles.at[pl.ds(part * i, part)], a.at[pl.ds(part * i, part)], tile_sem.at[i]
        )
        for i in range(4)
    ]
    for copy in tile_copies:
        copy.start()

    barrier = pltpu.get_barrier_semaphore()

    def greet(device):
        pl.semaphore_signal(barrier, inc=1, device_id=device, device_id_type=MESH)

    each(Y, lambda m: greet(y_device(y_peer(m))))
    each(U, lambda m: greet(u_device(u_peer(m))))
    each(Z, lambda m: greet(z_device(z_peer(m))))

    lane = lax.broadcasted_iota(jnp.int32, (TS, TS), 1)
    sub = lax.broadcasted_iota(jnp.int32, (TS, TS), 0)
    pos = rows_v[...] * CT + cols_v[...]
    pos = jnp.where(lane[:1] < count_s[0], pos, -1)
    pos_t = jnp.broadcast_to(pos, (TS, TS)).T
    inv_v[...] = jnp.full((8, TS), SLOTS, jnp.int32)
    for h in range(2):
        hit = pos_t == lane + TS * h
        inv_v[pl.ds(h, 1), :] = SLOTS + jnp.sum(
            jnp.where(hit, sub - SLOTS, 0), axis=0, keepdims=True
        )
    inv_copy = pltpu.make_async_copy(inv_v, inv_s, inv_sem)
    inv_copy.start()

    def slot_at(r, c):
        return inv_s[r // 2, (r % 2) * CT + c]

    own = sketch[...].astype(F32)
    xf[pl.ds(0, KROWS), :] = own
    xf[pl.ds(KROWS, KROWS), :] = own
    low = lax.broadcasted_iota(jnp.int32, (8, TS), 0) < KROWS
    for cc in range(CT // 4):
        pieces = [xf[:, pl.ds(TS * (4 * cc + i), TS)] for i in range(4)]
        block = jnp.concatenate(
            [jnp.where(low, pieces[0], pieces[1]), jnp.where(low, pieces[2], pieces[3])], axis=0
        )
        gath[row, pl.ds(16 * cc, 16), :] = block.astype(BF16)

    pl.semaphore_wait(barrier, Y + U + Z - 3)

    def block_copy(d, target):
        return pltpu.make_async_remote_copy(
            src_ref=gath.at[d],
            dst_ref=gath.at[d],
            send_sem=ag_send,
            recv_sem=ag_recv.at[d],
            device_id=(target, z),
            device_id_type=MESH,
        )

    def sibling_send(d):
        block_copy(d, row + 1 - 2 * core).start()

    def arrived(d):
        block_copy(d, row + 1 - 2 * core).wait_recv()

    def hops(n, way):
        return n // 2 if way > 0 else n // 2 - 1

    def plan(which):
        if which == 0:
            n_p, n_s, a_p, a_s = X, Y, x, y

            def rid(p, s):
                return (p * Y + s) * 2
        else:
            n_p, n_s, a_p, a_s = Y, X, y, x

            def rid(p, s):
                return (s * Y + p) * 2 + 1

        sign_p = 1 - 2 * lax.rem(a_s, 2)

        def origin_p(way, dist):
            return wrap(a_p - way * sign_p * dist, n_p)

        def p_target(way):
            return rid(wrap(a_p + way * sign_p, n_p), a_s)

        def s_target(sign_s, way):
            return rid(a_p, wrap(a_s + way * sign_s, n_s))

        def first(o_p, d, onward):
            for way in onward:
                block_copy(d, p_target(way)).start()
            sign_s = 1 - 2 * lax.rem(o_p, 2)
            for way in (1, -1):
                if hops(n_s, way) >= 1:
                    block_copy(d, s_target(sign_s, way)).start()
            sibling_send(d)

        def start():
            first(a_p, row, [way for way in (1, -1) if hops(n_p, way) >= 1])

        def wave(t):
            sources = [(1, 0)]
            for way in (1, -1):
                for dist in range(1, hops(n_p, way) + 1):
                    sources.append((way, dist))
                    if dist == t:
                        o_p = origin_p(way, dist)
                        d = rid(o_p, a_s)
                        arrived(d)
                        first(o_p, d, [way] if dist < hops(n_p, way) else [])
            for way_p, dist_p in sources:
                dist = t - dist_p
                for way in (1, -1):
                    if not 1 <= dist <= hops(n_s, way):
                        continue
                    o_p = origin_p(way_p, dist_p)
                    sign_s = 1 - 2 * lax.rem(o_p, 2)
                    d = rid(o_p, wrap(a_s - way * sign_s * dist, n_s))
                    arrived(d)
                    if dist < hops(n_s, way):
                        block_copy(d, s_target(sign_s, way)).start()
                    sibling_send(d)

        return start, wave

    def gather_step(t):
        for which in (0, 1):

            @pl.when(core == which)
            def _(which=which):
                start, wave = plan(which)
                if t == 0:
                    start()
                else:
                    wave(t)

    gather_step(0)

    a[SLOTS] = jnp.zeros((TS, TS), BF16)
    logm[SLOTS] = jnp.zeros((TS, TS), BF16)
    inv_copy.wait()
    for copy in tile_copies:
        copy.wait()
    rowbuf[...] = jnp.zeros((8, TS), F32)
    for r in range(RT):

        def add(c, total, r=r):
            tile = a[slot_at(r, c)].astype(F32)
            columns = jnp.sum(tile.reshape(TS // 8, 8, TS), axis=0)
            if r == 0:
                colpart[c] = columns
            else:
                colpart[c] += columns
            return total + tile

        total = lax.fori_loop(0, CT, add, jnp.zeros((TS, TS), F32))
        rowbuf[pl.ds(r, 1), :] = jnp.sum(total.T, axis=0, keepdims=True)
    colsrc[...] = jnp.sum(colpart[...], axis=1).reshape(Y, CT // Y, TS)

    def small(phase, slot, src, dst, device):
        return pltpu.make_async_remote_copy(
            src_ref=src,
            dst_ref=dst,
            send_sem=small_send.at[phase],
            recv_sem=small_recv.at[phase, slot],
            device_id=device,
            device_id_type=MESH,
        )

    def send_y(phase, src, dst):
        each(Y, lambda m: small(phase, y, src(y_peer(m)), dst.at[y], y_device(y_peer(m))).start())

    def send_u(phase, src, dst):
        each(U, lambda m: small(phase, u, src(u_peer(m)), dst.at[u], u_device(u_peer(m))).start())

    def send_z(phase, src, dst):
        each(Z, lambda m: small(phase, z, src(z_peer(m)), dst.at[z], z_device(z_peer(m))).start())

    def recv_y(phase, dst):
        each(Y, lambda m: small(phase, y_peer(m), dst.at[y_peer(m)], dst.at[y_peer(m)], y_device(y_peer(m))).wait_recv())

    def recv_u(phase, dst):
        each(U, lambda m: small(phase, u_peer(m), dst.at[u_peer(m)], dst.at[u_peer(m)], u_device(u_peer(m))).wait_recv())

    def recv_z(phase, dst):
        each(Z, lambda m: small(phase, z_peer(m), dst.at[z_peer(m)], dst.at[z_peer(m)], z_device(z_peer(m))).wait_recv())

    def sent(phase, dst):
        view = dst.at[pl.ds(0, 7)]
        small(phase, 0, view, view, z_device(z_peer(1))).wait_send()

    send_z(0, lambda v: rowbuf, zrow)
    send_y(1, lambda v: colsrc.at[v], ycol)
    zrow[z] = rowbuf[...]
    ycol[y] = colsrc[y]
    gather_step(1)
    recv_z(0, zrow)
    recv_y(1, ycol)
    row_sum = jnp.sum(zrow[...], axis=0)
    xdeg[u, pl.ds(0, 8), :] = jnp.sum(ycol[...], axis=0)
    xdeg[u, pl.ds(8, 8), :] = jnp.broadcast_to(jnp.sum(row_sum), (8, TS))
    send_u(2, lambda v: xdeg.at[u], xdeg)
    gather_step(2)
    recv_u(2, xdeg)
    ydeg[y] = jnp.sum(xdeg[...], axis=0)
    send_y(3, lambda v: ydeg.at[y], ydeg)
    gather_step(3)
    recv_y(3, ydeg)
    cinv[...] = 1.0 / (1.0 + ydeg[:, pl.ds(0, 8), :].reshape(CT, TS))
    volume = jnp.sum(ydeg[:, pl.ds(8, 8), :], axis=0)
    scale = volume / (1.0 + row_sum)
    for r in range(RT):
        rscale[r] = jnp.broadcast_to(scale[r : r + 1], (TS, TS)).T

    def log_step(s, carry):
        tile = a[s].astype(F32)
        ratio = tile * rscale[rows_s[s]] * cinv[pl.ds(cols_s[s], 1), :]
        logm[s] = jnp.log(jnp.maximum(ratio, 1.0)).astype(BF16)
        return carry

    lax.fori_loop(0, SLOTS // 2, log_step, 0)
    gather_step(4)
    lax.fori_loop(SLOTS // 2, SLOTS, log_step, 0)
    gather_step(5)
    gather_step(6)

    def from_sibling(i, carry):
        arrived(2 * i + 1 - core)
        return carry

    lax.fori_loop(0, ROW // 2, from_sibling, 0)

    def quad(i, carry):
        q, cc = i // (CT // 4), lax.rem(i, CT // 4)
        start = pl.multiple_of(16 * cc, 16)
        parts = [gath[4 * q + j, pl.ds(start, 16), :].astype(F32) for j in range(4)]
        for half in range(2):
            f = [p[8 * half : 8 * half + 8] for p in parts]
            g = [pltpu.roll(v, 4, 0) for v in f]
            first = [jnp.where(low, f[0], g[1]), jnp.where(low, f[2], g[3])]
            second = [jnp.where(low, g[0], f[1]), jnp.where(low, g[2], f[3])]
            for j, pair in enumerate((first, second)):
                weights[4 * cc + 2 * half + j, pl.ds(pl.multiple_of(16 * q, 16), 16), :] = (
                    jnp.concatenate(pair, axis=0).astype(BF16)
                )
        return carry

    lax.fori_loop(0, ROW // 4 * (CT // 4), quad, 0)

    acc[...] = jnp.zeros((OWN, K), F32)

    def product(i, carry):
        right = jnp.concatenate([weights[2 * i], weights[2 * i + 1]], axis=1)
        for r in range(RT):
            left = jnp.concatenate(
                [logm[slot_at(r, 2 * i)], logm[slot_at(r, 2 * i + 1)]], axis=1
            )
            acc[pl.ds(TS * r, TS), :] += lax.dot_general(
                left, right, NT_DIMS, preferred_element_type=F32
            )
        return carry

    lax.fori_loop(0, CT // 2, product, 0)

    psend[...] = acc[...].reshape(Z, SHARE, K).astype(BF16)
    send_z(4, lambda v: psend.at[v], precv)
    precv[z] = jnp.zeros((SHARE, K), BF16)
    recv_z(4, precv)
    result = acc[pl.ds(pl.multiple_of(z * SHARE, SHARE), SHARE), :]
    for i in range(Z):
        result = result + precv[i].astype(F32)
    embed[...] = result

    local_gram = lax.dot_general(
        result,
        result,
        (((0,), (0,)), ((), ())),
        precision=lax.Precision.HIGHEST,
        preferred_element_type=F32,
    ) * (1.0 / NR)
    gsrc[...] = local_gram.reshape(Z, K // Z, K)
    send_z(5, lambda v: gsrc.at[v], gz)
    gz[z] = gsrc[z]
    recv_z(5, gz)
    mine = jnp.sum(gz[...], axis=0)
    g64[pl.ds(0, 4)] = mine[:, :TS].reshape(4, 8, TS)
    g64[pl.ds(4, 4)] = mine[:, TS:].reshape(4, 8, TS)
    send_y(6, lambda v: g64.at[v], gy)
    gy[y] = g64[y]
    recv_y(6, gy)
    gx[u] = jnp.sum(gy[...], axis=0)
    send_u(7, lambda v: gx.at[u], gx)
    recv_u(7, gx)
    gfull[y] = jnp.sum(gx[...], axis=0)
    send_y(8, lambda v: gfull.at[y], gfull)
    recv_y(8, gfull)
    send_z(9, lambda v: gfull, gfin)
    gfin[z] = gfull[...]
    recv_z(9, gfin)
    for i in range(Z):
        gram[pl.ds(32 * i, 32), pl.ds(0, TS)] = gfin[i, pl.ds(0, 4)].reshape(32, TS)
        gram[pl.ds(32 * i, 32), pl.ds(TS, TS)] = gfin[i, pl.ds(4, 4)].reshape(32, TS)

    sent(0, zrow)
    sent(1, ycol)
    sent(2, xdeg)
    sent(3, ydeg)
    sent(4, precv)
    sent(5, gz)
    sent(6, gy)
    sent(7, gx)
    sent(8, gfull)
    sent(9, gfin)
    gone = gath.at[pl.ds(0, ROW - 1)]
    pltpu.make_async_remote_copy(
        src_ref=gone,
        dst_ref=gone,
        send_sem=ag_send,
        recv_sem=ag_recv.at[0],
        device_id=(row + 1 - 2 * core, z),
        device_id_type=MESH,
    ).wait_send()


def local(tile_values, tile_rows, tile_cols, tile_count, sketch):
    vmem = pl.BlockSpec(memory_space=pltpu.VMEM)
    smem = pl.BlockSpec(memory_space=pltpu.SMEM)
    scratch = [
        pltpu.VMEM((SLOTS + 1, TS, TS), BF16),
        pltpu.VMEM((SLOTS + 1, TS, TS), BF16),
        pltpu.VMEM((ROW, CT * KROWS, TS), BF16),
        pltpu.VMEM((CT, K, TS), BF16),
        pltpu.VMEM((OWN, K), F32),
        pltpu.VMEM((8, CT * TS), F32),
        pltpu.VMEM((8, TS), jnp.int32),
        pltpu.SMEM((8, TS), jnp.int32),
        pltpu.VMEM((CT, 8, TS), F32),
        pltpu.VMEM((Y, CT // Y, TS), F32),
        pltpu.VMEM((Y, 8, TS), F32),
        pltpu.VMEM((8, TS), F32),
        pltpu.VMEM((Z, 8, TS), F32),
        pltpu.VMEM((U, 16, TS), F32),
        pltpu.VMEM((Y, 16, TS), F32),
        pltpu.VMEM((RT, TS, TS), F32),
        pltpu.VMEM((CT, TS), F32),
        pltpu.VMEM((Z, SHARE, K), BF16),
        pltpu.VMEM((Z, SHARE, K), BF16),
        pltpu.VMEM((Z, K // Z, K), F32),
        pltpu.VMEM((Z, K // Z, K), F32),
        pltpu.VMEM((Y, 8, TS), F32),
        pltpu.VMEM((Y, 8, TS), F32),
        pltpu.VMEM((U, 8, TS), F32),
        pltpu.VMEM((Y, 8, TS), F32),
        pltpu.VMEM((Z, Y, 8, TS), F32),
        pltpu.SemaphoreType.DMA((4,)),
        pltpu.SemaphoreType.DMA,
        pltpu.SemaphoreType.DMA,
        pltpu.SemaphoreType.DMA((ROW,)),
        pltpu.SemaphoreType.DMA((10,)),
        pltpu.SemaphoreType.DMA((10, 8)),
    ]
    return pl.pallas_call(
        kernel,
        out_shape=(
            jax.ShapeDtypeStruct((SHARE, K), F32),
            jax.ShapeDtypeStruct((K, K), F32),
        ),
        in_specs=[vmem, vmem, smem, smem, smem, vmem, pl.BlockSpec(memory_space=pl.ANY)],
        out_specs=(vmem, vmem),
        scratch_shapes=scratch,
        compiler_params=pltpu.CompilerParams(
            collective_id=0, has_side_effects=True, vmem_limit_bytes=48 * 1024 * 1024
        ),
    )(
        tile_rows.reshape(1, SLOTS),
        tile_cols.reshape(1, SLOTS),
        tile_rows,
        tile_cols,
        tile_count,
        sketch,
        tile_values,
    )


def solution(mesh):
    placed = (
        P(("row", "col"), None, None),
        P(("row", "col")),
        P(("row", "col")),
        P(("row", "col")),
        P("row", "col"),
    )
    return jax.shard_map(
        local, mesh=mesh, in_specs=placed, out_specs=(P(("row", "col"), None), P()), check_vma=False
    )
```

time: 721 us -> 109 us (0.15)
  blocking collectives: 364 us -> 0 us
  waiting for transfers between devices: 287 us -> 0 us
  Pallas kernels: 0 us -> 102 us
  local copies, waits for them, and re-layouts: 30.1 us -> 5.66 us
  matrix products: 18.5 us -> 0 us
  between operations: 14.5 us -> 1.3 us
    psum x3 -> x0, blocking collectives: 364 us -> none  [the longest x1 245 us: local(): column_total_sum = lax.psum(col_part, 'row')]
    psum x2 -> x0, waiting for transfers between devices: 286 us -> none  [the longest x1 189 us: local(): gram = lax.psum(local_gram, 'row') / overall_row_count]
    pallas_call x0 -> x1, Pallas kernels: none -> 102 us  [local(): pl.pallas_call(kernel, out_shape=(jax.ShapeDtypeStruct((SHARE, K), F32),...]
    dot_general x9 -> x0, matrix products: 18.5 us -> none  [the longest x3 7.78 us: step(): jnp.einsum('tr,tik->rik', onehot, contrib, precision=lax.Precision.HIGHEST)]
    gather x9 -> x0, local copies, waits for them, and re-layouts: 12.2 us -> none  [the longest x3 8.81 us: step(): picked = jnp.take(sketch3, cols, axis=1)]
    reshape x1 -> x0, local copies, waits for them, and re-layouts: 8.44 us -> none  [local(): sketch3 = gathered.reshape(width, CT, edge)]
    while x2 -> x0, local copies, waits for them, and re-layouts: 7.72 us -> none  [local(): lax.fori_loop(0, nblocks, step, start_acc).reshape(own_rows, width)]
  transfers between devices with their start and end apart: 3 -> 0, of which waited for: 2 -> 0; matrix products, arithmetic and copies ran while one was open for 1% -> 0% of each run, Pallas kernels for 0% -> 0%
where the time goes in v1:
time: 109 us
  Pallas kernels  102 us (94%)
  local copies, waits for them, and re-layouts  5.66 us (5%)
  between operations  1.3 us (1%)
    pallas_call x1, Pallas kernels, local(): pl.pallas_call(kernel, out_shape=(jax.ShapeDtypeStruct((SHARE, K), F32),...  102 us
    unnamed x10, local copies, waits for them, and re-layouts  5.66 us

profile of v1, /device:TPU:1, one launch (start us, length us, event | category | flops | bytes accessed | tf_op | source)
XLA Modules:
  0.0 108.6 jit_solution(9471415479922968013)
XLA Ops:
  1.3 0.0 copy-start
  1.3 2.2 %copy-done = bf16[128,128,128]{2,1,0:T(8,128)(2,1)S(1)} copy-done((bf16[128,128,128]{2,1,0:T(8,128)(2,1)S(1)}, bf16[128,128,128]{2,1,0:T(8,128)(2,1)}, u32[]{:S(2)}) %copy-start) | copy-done | bytes 4194328
  3.5 0.0 copy-start.1
  3.5 0.8 copy-done.1
  4.3 0.0 copy-start.2
  4.3 0.7 copy-done.2
  5.0 0.0 copy-start.3
  5.0 0.7 copy-done.3
  5.6 101.6 %shard_map.68 = (f32[64,256]{1,0:T(8,128)S(1)}, f32[256,256]{1,0:T(8,128)S(1)}) custom-call(s32[1,128]{1,0:T(1,128)S(1)} %bitcast.2, s32[1,128]{1,0:T(1,128)S(1)} %bitcast.3, s32[128]{0:T(128)S(1)} %copy-done.2, s32[128]{0:T(128)S(1)} %copy-done.3, s32[1]{0:T(128)S(6)} %copy.9.count_s, bf16[4,8192]{1,0:T(4,128)(2,1)S(1)} %copy-done.1, ...), custom_call_target="tpu_custom_call" | custom-call | tf_op jit(solution)/shard_map/pallas_call | solution.py:471
  107.2 0.6 copy.10
  107.9 0.7 copy.11
Async XLA Ops:
  1.3 2.2 %copy-start = (bf16[128,128,128]{2,1,0:T(8,128)(2,1)S(1)}, bf16[128,128,128]{2,1,0:T(8,128)(2,1)}, u32[]{:S(2)}) copy-start(bf16[128,128,128]{2,1,0:T(8,128)(2,1)} %tiles.1) | copy-start | bytes 12582916
  3.5 0.8 copy-start.1
  4.3 0.7 copy-start.2
  5.0 0.7 copy-start.3

commit v2 on v1

v2 whole, which is shorter than its diff:
```python
import jax
import jax.numpy as jnp
from jax import lax
from jax.experimental import pallas as pl
from jax.experimental.pallas import tpu as pltpu
from jax.sharding import PartitionSpec as P

MESH = pl.DeviceIdType.MESH
F32 = jnp.float32
BF16 = jnp.bfloat16

TS = 128
RT = 4
CT = 64
SLOTS = 128
K = 256
X, Y, Z = 4, 8, 8
U = 2 * X
ROW = X * Y * 2
NR = ROW * RT * TS
OWN = RT * TS
SHARE = OWN // Z
KROWS = 4
H = 64
GROWS = 5 * H // U
NT_DIMS = (((1,), (1,)), ((), ()))


def wrap(value, n):
    return lax.rem(value + 4 * n, n)


def each(n, f):
    def step(m, carry):
        f(m)
        return carry

    lax.fori_loop(1, n, step, 0)


def kernel(
    rows_h,
    cols_h,
    count_h,
    sketch_h,
    tiles,
    embed,
    gram,
    a,
    logm,
    gath,
    weights,
    acc,
    sketch,
    xf,
    rows_v,
    cols_v,
    rows_s,
    cols_s,
    count_s,
    inv_v,
    inv_s,
    colpart,
    colsrc,
    ucol,
    rowbuf,
    zrow,
    ydeg,
    udeg,
    rscale,
    cinv,
    psend,
    precv,
    gsrc,
    gu,
    gy,
    gz,
    gfin,
    tile_sem,
    in_sem,
    inv_sem,
    ag_send,
    ag_recv,
    small_send,
    small_recv,
):
    row = lax.axis_index("row")
    z = lax.axis_index("col")
    core = lax.rem(row, 2)
    y = lax.rem(row // 2, Y)
    x = row // (2 * Y)
    u = 2 * x + core

    def y_peer(m):
        return wrap(y + m, Y)

    def u_peer(m):
        return wrap(u + m, U)

    def z_peer(m):
        return wrap(z + m, Z)

    def rid(xx, yy):
        return (xx * Y + yy) * 2 + core

    def y_device(v):
        return (rid(x, v), z)

    def u_device(v):
        return ((v // 2 * Y + y) * 2 + lax.rem(v, 2), z)

    def z_device(v):
        return (row, v)

    barrier = pltpu.get_barrier_semaphore()

    def greet(device):
        pl.semaphore_signal(barrier, inc=1, device_id=device, device_id_type=MESH)

    each(Y, lambda m: greet(y_device(y_peer(m))))
    each(U, lambda m: greet(u_device(u_peer(m))))
    each(Z, lambda m: greet(z_device(z_peer(m))))

    in_copies = [
        pltpu.make_async_copy(src, dst, in_sem.at[i])
        for i, (src, dst) in enumerate(
            (
                (sketch_h, sketch),
                (rows_h, rows_v),
                (cols_h, cols_v),
                (count_h, count_s),
                (rows_h, rows_s),
                (cols_h, cols_s),
            )
        )
    ]
    for copy in in_copies:
        copy.start()
    part = SLOTS // 4
    tile_copies = [
        pltpu.make_async_copy(
            tiles.at[pl.ds(part * i, part)], a.at[pl.ds(part * i, part)], tile_sem.at[i]
        )
        for i in range(4)
    ]
    for copy in tile_copies:
        copy.start()

    in_copies[0].wait()
    own = sketch[...].astype(F32)
    xf[pl.ds(0, KROWS), :] = own
    xf[pl.ds(KROWS, KROWS), :] = own
    low = lax.broadcasted_iota(jnp.int32, (8, TS), 0) < KROWS
    for cc in range(CT // 4):
        pieces = [xf[:, pl.ds(TS * (4 * cc + i), TS)] for i in range(4)]
        block = jnp.concatenate(
            [jnp.where(low, pieces[0], pieces[1]), jnp.where(low, pieces[2], pieces[3])], axis=0
        )
        gath[row, pl.ds(16 * cc, 16), :] = block.astype(BF16)

    for copy in in_copies[1:]:
        copy.wait()
    lane = lax.broadcasted_iota(jnp.int32, (TS, TS), 1)
    sub = lax.broadcasted_iota(jnp.int32, (TS, TS), 0)
    pos = rows_v[...] * CT + cols_v[...]
    pos = jnp.where(lane[:1] < count_s[0], pos, -1)
    pos_t = jnp.broadcast_to(pos, (TS, TS)).T
    inv_v[...] = jnp.full((8, TS), SLOTS, jnp.int32)
    for h in range(2):
        hit = pos_t == lane + TS * h
        inv_v[pl.ds(h, 1), :] = SLOTS + jnp.sum(
            jnp.where(hit, sub - SLOTS, 0), axis=0, keepdims=True
        )
    inv_copy = pltpu.make_async_copy(inv_v, inv_s, inv_sem)
    inv_copy.start()

    def slot_at(r, c):
        return inv_s[r // 2, (r % 2) * CT + c]

    pl.semaphore_wait(barrier, Y + U + Z - 3)

    def block_copy(d, target):
        return pltpu.make_async_remote_copy(
            src_ref=gath.at[d],
            dst_ref=gath.at[d],
            send_sem=ag_send,
            recv_sem=ag_recv.at[d],
            device_id=(target, z),
            device_id_type=MESH,
        )

    sibling = row + 1 - 2 * core

    def arrived(d):
        block_copy(d, sibling).wait_recv()

    def along_x(d):
        block_copy(d, rid(wrap(x + 1, X), y)).start()
        block_copy(d, rid(wrap(x - 1, X), y)).start()

    def to_sibling(d):
        block_copy(d, sibling).start()

    def near(m):
        yy = y_peer(m)
        sign = 1 - 2 * lax.rem(yy, 2)
        relayed = rid(wrap(x - sign, X), yy)
        other = rid(wrap(x + sign, X), yy)
        arrived(relayed)
        block_copy(relayed, rid(wrap(x + sign, X), y)).start()
        to_sibling(relayed)
        arrived(other)
        to_sibling(other)

    def far(m):
        d = rid(wrap(x + 2, X), y_peer(m))
        arrived(d)
        to_sibling(d)

    def by_y(m):
        d = rid(x, y_peer(m))
        arrived(d)
        along_x(d)
        if m not in (-3, 4):
            block_copy(d, rid(x, y_peer(-1 if m > 0 else 1))).start()
        to_sibling(d)

    rings = ((0,), (1, -1), (2, -2), (3, -3), (4,))

    def gather_step(t):
        if t == 0:
            along_x(row)
            for m in (1, -1):
                block_copy(row, rid(x, y_peer(m))).start()
            to_sibling(row)
            return
        for f, i in ((by_y, t), (near, t - 1), (far, t - 2)):
            if 0 <= i < len(rings):
                for m in rings[i]:
                    if f is not by_y or m != 0:
                        f(m)

    gather_step(0)

    a[SLOTS] = jnp.zeros((TS, TS), BF16)
    logm[SLOTS] = jnp.zeros((TS, TS), BF16)
    inv_copy.wait()
    for copy in tile_copies:
        copy.wait()
    rowbuf[...] = jnp.zeros((8, TS), F32)
    for r in range(RT):

        def add(c, total, r=r):
            tile = a[slot_at(r, c)].astype(F32)
            columns = jnp.sum(tile.reshape(TS // 8, 8, TS), axis=0)
            if r == 0:
                colpart[c] = columns
            else:
                colpart[c] += columns
            return total + tile

        total = lax.fori_loop(0, CT, add, jnp.zeros((TS, TS), F32), unroll=8)
        rowbuf[pl.ds(r, 1), :] = jnp.sum(total.T, axis=0, keepdims=True)
    colsrc[...] = jnp.sum(colpart[...], axis=1).reshape(U, CT // U, TS)

    def small(phase, slot, src, dst, device):
        return pltpu.make_async_remote_copy(
            src_ref=src,
            dst_ref=dst,
            send_sem=small_send.at[phase],
            recv_sem=small_recv.at[phase, slot],
            device_id=device,
            device_id_type=MESH,
        )

    def send_y(phase, src, dst):
        each(Y, lambda m: small(phase, y, src(y_peer(m)), dst.at[y], y_device(y_peer(m))).start())

    def send_u(phase, src, dst):
        each(U, lambda m: small(phase, u, src(u_peer(m)), dst.at[u], u_device(u_peer(m))).start())

    def send_z(phase, src, dst):
        each(Z, lambda m: small(phase, z, src(z_peer(m)), dst.at[z], z_device(z_peer(m))).start())

    def recv_y(phase, dst):
        each(Y, lambda m: small(phase, y_peer(m), dst.at[y_peer(m)], dst.at[y_peer(m)], y_device(y_peer(m))).wait_recv())

    def recv_u(phase, dst):
        each(U, lambda m: small(phase, u_peer(m), dst.at[u_peer(m)], dst.at[u_peer(m)], u_device(u_peer(m))).wait_recv())

    def recv_z(phase, dst):
        each(Z, lambda m: small(phase, z_peer(m), dst.at[z_peer(m)], dst.at[z_peer(m)], z_device(z_peer(m))).wait_recv())

    def sent(phase, dst):
        view = dst.at[pl.ds(0, 7)]
        small(phase, 0, view, view, z_device(z_peer(1))).wait_send()

    send_z(0, lambda v: rowbuf, zrow)
    send_u(1, lambda v: colsrc.at[v], ucol)
    zrow[z] = rowbuf[...]
    ucol[u] = colsrc[u]
    gather_step(1)
    recv_u(1, ucol)
    recv_z(0, zrow)
    row_sum = jnp.sum(zrow[...], axis=0)
    ydeg[y, pl.ds(0, 8), :] = jnp.sum(ucol[...], axis=0)
    ydeg[y, pl.ds(8, 8), :] = row_sum
    send_y(2, lambda v: ydeg.at[y], ydeg)
    gather_step(2)
    recv_y(2, ydeg)
    udeg[u] = jnp.sum(ydeg[...], axis=0)
    send_u(3, lambda v: udeg.at[u], udeg)
    gather_step(3)
    recv_u(3, udeg)
    cinv[...] = 1.0 / (1.0 + udeg[:, pl.ds(0, 8), :].reshape(CT, TS))
    volume = jnp.sum(jnp.sum(udeg[:, pl.ds(8, 8), :], axis=0), axis=(0, 1), keepdims=True)
    scale = volume / (1.0 + row_sum)
    for r in range(RT):
        rscale[r] = jnp.broadcast_to(scale[r : r + 1], (TS, TS)).T

    def log_step(s, carry):
        tile = a[s].astype(F32)
        ratio = tile * rscale[rows_s[0, s]] * cinv[pl.ds(cols_s[0, s], 1), :]
        logm[s] = jnp.log(jnp.maximum(ratio, 1.0)).astype(BF16)
        return carry

    lax.fori_loop(0, SLOTS // 2, log_step, 0, unroll=4)
    gather_step(4)
    lax.fori_loop(SLOTS // 2, SLOTS, log_step, 0, unroll=4)

    def arrange(xx):
        def from_sibling(i, carry):
            arrived((xx * Y + i) * 2 + 1 - core)
            return carry

        lax.fori_loop(0, Y, from_sibling, 0)

        def quad(i, carry):
            q, cc = xx * (Y // 2) + i // (CT // 4), lax.rem(i, CT // 4)
            start = pl.multiple_of(16 * cc, 16)
            parts = [gath[4 * q + j, pl.ds(start, 16), :].astype(F32) for j in range(4)]
            for half in range(2):
                f = [p[8 * half : 8 * half + 8] for p in parts]
                g = [pltpu.roll(v, 4, 0) for v in f]
                first = [jnp.where(low, f[0], g[1]), jnp.where(low, f[2], g[3])]
                second = [jnp.where(low, g[0], f[1]), jnp.where(low, g[2], f[3])]
                for j, pair in enumerate((first, second)):
                    weights[4 * cc + 2 * half + j, pl.ds(pl.multiple_of(16 * q, 16), 16), :] = (
                        jnp.concatenate(pair, axis=0).astype(BF16)
                    )
            return carry

        lax.fori_loop(0, Y // 2 * (CT // 4), quad, 0, unroll=4)

    arrange(x)
    gather_step(5)
    arrange(wrap(x + 1, X))
    arrange(wrap(x - 1, X))
    gather_step(6)
    arrange(wrap(x + 2, X))

    depth = 16
    acc[...] = jnp.zeros((OWN, K), F32)
    for half in range(2):

        def product(i, carry, half=half):
            right = jnp.concatenate([weights[depth * i + t] for t in range(depth)], axis=1)
            left = jnp.concatenate(
                [
                    jnp.concatenate(
                        [logm[slot_at(r, depth * i + t)] for t in range(depth)], axis=1
                    )
                    for r in (2 * half, 2 * half + 1)
                ],
                axis=0,
            )
            acc[pl.ds(OWN // 2 * half, OWN // 2), :] += lax.dot_general(
                left, right, NT_DIMS, preferred_element_type=F32
            )
            return carry

        lax.fori_loop(0, CT // depth, product, 0)
        block = acc[pl.ds(OWN // 2 * half, OWN // 2), :]
        psend[pl.ds(Z // 2 * half, Z // 2)] = block.reshape(Z // 2, SHARE, K).astype(BF16)
        for i in range(Z // 2):
            v = Z // 2 * half + i

            @pl.when(z != v)
            def _(v=v):
                small(4, z, psend.at[v], precv.at[z], z_device(v)).start()

    precv[z] = jnp.zeros((SHARE, K), BF16)
    result = acc[pl.ds(pl.multiple_of(z * SHARE, SHARE), SHARE), :]
    recv_z(4, precv)
    for i in range(Z):
        result = result + precv[i].astype(F32)
    embed[...] = result

    local_gram = lax.dot_general(
        result,
        result,
        (((0,), (0,)), ((), ())),
        precision=lax.Precision.HIGHEST,
        preferred_element_type=F32,
    ) * (1.0 / NR)
    left = lax.broadcasted_iota(jnp.int32, (H, TS), 1) < H
    corner = jnp.where(
        left, pltpu.roll(local_gram[3 * H :, TS:], H, 1), local_gram[H : 2 * H, :TS]
    )
    gsrc[...] = jnp.concatenate(
        [local_gram[:H, :TS], local_gram[: 3 * H, TS:], corner], axis=0
    ).reshape(U, GROWS, TS)
    send_u(5, lambda v: gsrc.at[v], gu)
    gu[u] = gsrc[u]
    recv_u(5, gu)
    gy[y] = jnp.sum(gu[...], axis=0)
    send_y(6, lambda v: gy.at[y], gy)
    recv_y(6, gy)
    gz[z] = jnp.sum(gy[...], axis=0)
    send_z(7, lambda v: gz.at[z], gz)
    recv_z(7, gz)
    gfin[u] = jnp.sum(gz[...], axis=0)
    send_u(8, lambda v: gfin.at[u], gfin)
    recv_u(8, gfin)
    packed = gfin[...].reshape(5 * H, TS)
    corner = packed[4 * H :]
    mirrored = (lax.broadcasted_iota(jnp.int32, (TS, TS), 0) >= H) & (
        lax.broadcasted_iota(jnp.int32, (TS, TS), 1) < H
    )
    first = jnp.concatenate([packed[:H], corner], axis=0)
    gram[pl.ds(0, TS), pl.ds(0, TS)] = jnp.where(mirrored, first.T, first)
    across = packed[H : 3 * H]
    gram[pl.ds(0, TS), pl.ds(TS, TS)] = across
    gram[pl.ds(TS, TS), pl.ds(0, TS)] = across.T
    last = jnp.concatenate([packed[3 * H : 4 * H], pltpu.roll(corner, H, 1)], axis=0)
    gram[pl.ds(TS, TS), pl.ds(TS, TS)] = jnp.where(mirrored, last.T, last)

    sent(0, zrow)
    sent(1, ucol)
    sent(2, ydeg)
    sent(3, udeg)
    sent(4, precv)
    sent(5, gu)
    sent(6, gy)
    sent(7, gz)
    sent(8, gfin)
    gone = gath.at[pl.ds(0, ROW - 1)]
    pltpu.make_async_remote_copy(
        src_ref=gone,
        dst_ref=gone,
        send_sem=ag_send,
        recv_sem=ag_recv.at[0],
        device_id=(sibling, z),
        device_id_type=MESH,
    ).wait_send()


def hand_over(embed, gram, embed_out, gram_out):
    embed_out[...] = embed[...]
    gram_out[...] = gram[...]


def local(tile_values, tile_rows, tile_cols, tile_count, sketch):
    vmem = pl.BlockSpec(memory_space=pltpu.VMEM)
    hbm = pl.BlockSpec(memory_space=pltpu.HBM)
    scratch = [
        pltpu.VMEM((SLOTS + 1, TS, TS), BF16),
        pltpu.VMEM((SLOTS + 1, TS, TS), BF16),
        pltpu.VMEM((ROW, CT * KROWS, TS), BF16),
        pltpu.VMEM((CT, K, TS), BF16),
        pltpu.VMEM((OWN, K), F32),
        pltpu.VMEM((KROWS, CT * TS), BF16),
        pltpu.VMEM((8, CT * TS), F32),
        pltpu.VMEM((1, SLOTS), jnp.int32),
        pltpu.VMEM((1, SLOTS), jnp.int32),
        pltpu.SMEM((1, SLOTS), jnp.int32),
        pltpu.SMEM((1, SLOTS), jnp.int32),
        pltpu.SMEM((1,), jnp.int32),
        pltpu.VMEM((8, TS), jnp.int32),
        pltpu.SMEM((8, TS), jnp.int32),
        pltpu.VMEM((CT, 8, TS), F32),
        pltpu.VMEM((U, CT // U, TS), F32),
        pltpu.VMEM((U, 8, TS), F32),
        pltpu.VMEM((8, TS), F32),
        pltpu.VMEM((Z, 8, TS), F32),
        pltpu.VMEM((Y, 16, TS), F32),
        pltpu.VMEM((U, 16, TS), F32),
        pltpu.VMEM((RT, TS, TS), F32),
        pltpu.VMEM((CT, TS), F32),
        pltpu.VMEM((Z, SHARE, K), BF16),
        pltpu.VMEM((Z, SHARE, K), BF16),
        pltpu.VMEM((U, GROWS, TS), F32),
        pltpu.VMEM((U, GROWS, TS), F32),
        pltpu.VMEM((Y, GROWS, TS), F32),
        pltpu.VMEM((Z, GROWS, TS), F32),
        pltpu.VMEM((U, GROWS, TS), F32),
        pltpu.SemaphoreType.DMA((4,)),
        pltpu.SemaphoreType.DMA((6,)),
        pltpu.SemaphoreType.DMA,
        pltpu.SemaphoreType.DMA,
        pltpu.SemaphoreType.DMA((ROW,)),
        pltpu.SemaphoreType.DMA((9,)),
        pltpu.SemaphoreType.DMA((9, 8)),
    ]
    embed, gram = pl.pallas_call(
        kernel,
        out_shape=(
            jax.ShapeDtypeStruct((SHARE, K), F32),
            jax.ShapeDtypeStruct((K, K), F32),
        ),
        in_specs=[hbm] * 5,
        out_specs=(vmem, vmem),
        scratch_shapes=scratch,
        compiler_params=pltpu.CompilerParams(
            collective_id=0, has_side_effects=True, vmem_limit_bytes=63 * 1024 * 1024
        ),
    )(
        tile_rows.reshape(1, SLOTS),
        tile_cols.reshape(1, SLOTS),
        tile_count,
        sketch,
        tile_values,
    )
    return pl.pallas_call(
        hand_over,
        out_shape=(
            jax.ShapeDtypeStruct((SHARE, K), F32),
            jax.ShapeDtypeStruct((K, K), F32),
        ),
        in_specs=[vmem] * 2,
        out_specs=(vmem, vmem),
    )(embed, gram)


def solution(mesh):
    placed = (
        P(("row", "col"), None, None),
        P(("row", "col")),
        P(("row", "col")),
        P(("row", "col")),
        P("row", "col"),
    )
    return jax.shard_map(
        local, mesh=mesh, in_specs=placed, out_specs=(P(("row", "col"), None), P()), check_vma=False
    )
```

time: 109 us -> 80.2 us (0.74)
  Pallas kernels: 102 us -> 78.8 us
  local copies, waits for them, and re-layouts: 5.66 us -> 0 us
    pallas_call x1, Pallas kernels: 102 us -> 77.1 us  [local(): pl.pallas_call(kernel, out_shape=(jax.ShapeDtypeStruct((SHARE, K), F32),...]
    unnamed x10 -> x0, local copies, waits for them, and re-layouts: 5.66 us -> none
    pallas_call x0 -> x1, Pallas kernels: none -> 1.72 us  [local(): pl.pallas_call(hand_over, out_shape=(jax.ShapeDtypeStruct((SHARE, K), F32...]
where the time goes in v2:
time: 80.2 us; the launch traced here: 80.1 us
  Pallas kernels  78.8 us (98%)
  between operations  1.28 us (2%)
    pallas_call x1, Pallas kernels, local(): pl.pallas_call(kernel, out_shape=(jax.ShapeDtypeStruct((SHARE, K), F32),...  77.1 us
    pallas_call x1, Pallas kernels, local(): pl.pallas_call(hand_over, out_shape=(jax.ShapeDtypeStruct((SHARE, K), F32...  1.72 us

profile of v2, /device:TPU:1, one launch (start us, length us, event | category | flops | bytes accessed | tf_op | source)
XLA Modules:
  0.0 80.1 jit_solution(10307102849902308556)
XLA Ops:
  1.3 77.1 %shard_map.68 = (f32[64,256]{1,0:T(8,128)}, f32[256,256]{1,0:T(8,128)}) custom-call(s32[1,128]{1,0:T(1,128)} %bitcast.2, s32[1,128]{1,0:T(1,128)} %bitcast.3, s32[1]{0:T(128)S(6)} %copy.7.count_h, bf16[4,8192]{1,0:T(4,128)(2,1)} %sketch_h.1, bf16[128,128,128]{2,1,0:T(8,128)(2,1)} %tiles.1), custom_call_target="tpu_custom_call" | custom-call | tf_op jit(solution)/shard_map/pallas_call | solution.py:505
  78.3 1.7 %shard_map.69 = (f32[64,256]{1,0:T(8,128)}, f32[256,256]{1,0:T(8,128)}) custom-call(f32[64,256]{1,0:T(8,128)} %get-tuple-element.4.embed, f32[256,256]{1,0:T(8,128)} %get-tuple-element.5.gram), custom_call_target="tpu_custom_call" | custom-call | tf_op jit(solution)/shard_map/pallas_call | solution.py:524

commit v3 on v2

--- a/solution.py
+++ b/solution.py
@@ -21,13 +21,19 @@
 OWN = RT * TS
 SHARE = OWN // Z
 KROWS = 4
-H = 64
-GROWS = 5 * H // U
+GROWS = 3 * TS // U
 NT_DIMS = (((1,), (1,)), ((), ()))
 
 
 def wrap(value, n):
     return lax.rem(value + 4 * n, n)
+
+
+def total_of(ref):
+    total = ref[0].astype(F32)
+    for i in range(1, ref.shape[0]):
+        total = total + ref[i].astype(F32)
+    return total
 
 
 def each(n, f):
@@ -35,7 +41,7 @@
         f(m)
         return carry
 
-    lax.fori_loop(1, n, step, 0)
+    lax.fori_loop(1, n, step, 0, unroll=True)
 
 
 def kernel(
@@ -80,6 +86,7 @@
     in_sem,
     inv_sem,
     ag_send,
+    sib_send,
     ag_recv,
     small_send,
     small_recv,
@@ -136,10 +143,12 @@
     ]
     for copy in in_copies:
         copy.start()
-    part = SLOTS // 4
+    quarter = SLOTS // 4
     tile_copies = [
         pltpu.make_async_copy(
-            tiles.at[pl.ds(part * i, part)], a.at[pl.ds(part * i, part)], tile_sem.at[i]
+            tiles.at[pl.ds(quarter * i, quarter)],
+            a.at[pl.ds(quarter * i, quarter)],
+            tile_sem.at[i],
         )
         for i in range(4)
     ]
@@ -177,7 +186,31 @@
     def slot_at(r, c):
         return inv_s[r // 2, (r % 2) * CT + c]
 
+
+    a[SLOTS] = jnp.zeros((TS, TS), BF16)
+    logm[SLOTS] = jnp.zeros((TS, TS), BF16)
+    inv_copy.wait()
+    for copy in tile_copies:
+        copy.wait()
+    rowbuf[...] = jnp.zeros((8, TS), F32)
+    for r in range(RT):
+
+        def add(c, total, r=r):
+            tile = a[slot_at(r, c)].astype(F32)
+            columns = jnp.sum(tile.reshape(TS // 8, 8, TS), axis=0)
+            if r == 0:
+                colpart[c] = columns
+            else:
+                colpart[c] += columns
+            return total + tile
+
+        total = lax.fori_loop(0, CT, add, jnp.zeros((TS, TS), F32), unroll=8)
+        rowbuf[pl.ds(r, 1), :] = jnp.sum(total.T, axis=0, keepdims=True)
+    colsrc[...] = jnp.sum(colpart[...], axis=1).reshape(U, CT // U, TS)
+
     pl.semaphore_wait(barrier, Y + U + Z - 3)
+
+    sibling = row + 1 - 2 * core
 
     def block_copy(d, target):
         return pltpu.make_async_remote_copy(
@@ -189,17 +222,37 @@
             device_id_type=MESH,
         )
 
-    sibling = row + 1 - 2 * core
+    def sibling_copy(d):
+        return pltpu.make_async_remote_copy(
+            src_ref=gath.at[d],
+            dst_ref=gath.at[d],
+            send_sem=sib_send,
+            recv_sem=ag_recv.at[d],
+            device_id=(sibling, z),
+            device_id_type=MESH,
+        )
 
     def arrived(d):
-        block_copy(d, sibling).wait_recv()
+        sibling_copy(d).wait_recv()
+
+    def to_sibling(d):
+        sibling_copy(d).start()
 
     def along_x(d):
         block_copy(d, rid(wrap(x + 1, X), y)).start()
         block_copy(d, rid(wrap(x - 1, X), y)).start()
 
-    def to_sibling(d):
-        block_copy(d, sibling).start()
+    def along_y(d, m):
+        for way in (1, -1):
+            if m == 0 or (way < 0 < m < Y // 2) or (way > 0 > m > 1 - Y // 2):
+                block_copy(d, rid(x, y_peer(way))).start()
+
+    def by_y(m):
+        d = rid(x, y_peer(m))
+        arrived(d)
+        along_y(d, m)
+        along_x(d)
+        to_sibling(d)
 
     def near(m):
         yy = y_peer(m)
@@ -217,21 +270,12 @@
         arrived(d)
         to_sibling(d)
 
-    def by_y(m):
-        d = rid(x, y_peer(m))
-        arrived(d)
-        along_x(d)
-        if m not in (-3, 4):
-            block_copy(d, rid(x, y_peer(-1 if m > 0 else 1))).start()
-        to_sibling(d)
-
     rings = ((0,), (1, -1), (2, -2), (3, -3), (4,))
 
     def gather_step(t):
         if t == 0:
             along_x(row)
-            for m in (1, -1):
-                block_copy(row, rid(x, y_peer(m))).start()
+            along_y(row, 0)
             to_sibling(row)
             return
         for f, i in ((by_y, t), (near, t - 1), (far, t - 2)):
@@ -240,28 +284,6 @@
                     if f is not by_y or m != 0:
                         f(m)
 
-    gather_step(0)
-
-    a[SLOTS] = jnp.zeros((TS, TS), BF16)
-    logm[SLOTS] = jnp.zeros((TS, TS), BF16)
-    inv_copy.wait()
-    for copy in tile_copies:
-        copy.wait()
-    rowbuf[...] = jnp.zeros((8, TS), F32)
-    for r in range(RT):
-
-        def add(c, total, r=r):
-            tile = a[slot_at(r, c)].astype(F32)
-            columns = jnp.sum(tile.reshape(TS // 8, 8, TS), axis=0)
-            if r == 0:
-                colpart[c] = columns
-            else:
-                colpart[c] += columns
-            return total + tile
-
-        total = lax.fori_loop(0, CT, add, jnp.zeros((TS, TS), F32), unroll=8)
-        rowbuf[pl.ds(r, 1), :] = jnp.sum(total.T, axis=0, keepdims=True)
-    colsrc[...] = jnp.sum(colpart[...], axis=1).reshape(U, CT // U, TS)
 
     def small(phase, slot, src, dst, device):
         return pltpu.make_async_remote_copy(
@@ -297,6 +319,7 @@
 
     send_z(0, lambda v: rowbuf, zrow)
     send_u(1, lambda v: colsrc.at[v], ucol)
+    gather_step(0)
     zrow[z] = rowbuf[...]
     ucol[u] = colsrc[u]
     gather_step(1)
@@ -352,49 +375,71 @@
 
         lax.fori_loop(0, Y // 2 * (CT // 4), quad, 0, unroll=4)
 
-    arrange(x)
-    gather_step(5)
-    arrange(wrap(x + 1, X))
-    arrange(wrap(x - 1, X))
-    gather_step(6)
-    arrange(wrap(x + 2, X))
-
     depth = 16
-    acc[...] = jnp.zeros((OWN, K), F32)
-    for half in range(2):
-
-        def product(i, carry, half=half):
-            right = jnp.concatenate([weights[depth * i + t] for t in range(depth)], axis=1)
+    mate = x + 1 - 2 * lax.rem(x, 2)
+    acc[...] = jnp.zeros((2, OWN, TS), F32)
+
+    def products(half, top):
+        def product(i, carry):
+            columns = pl.ds(pl.multiple_of(half * TS, TS), TS)
+            right = jnp.concatenate(
+                [weights[depth * i + t, columns, :] for t in range(depth)], axis=1
+            )
             left = jnp.concatenate(
                 [
                     jnp.concatenate(
                         [logm[slot_at(r, depth * i + t)] for t in range(depth)], axis=1
                     )
-                    for r in (2 * half, 2 * half + 1)
+                    for r in (2 * top, 2 * top + 1)
                 ],
                 axis=0,
             )
-            acc[pl.ds(OWN // 2 * half, OWN // 2), :] += lax.dot_general(
+            acc[half, pl.ds(OWN // 2 * top, OWN // 2), :] += lax.dot_general(
                 left, right, NT_DIMS, preferred_element_type=F32
             )
             return carry
 
         lax.fori_loop(0, CT // depth, product, 0)
-        block = acc[pl.ds(OWN // 2 * half, OWN // 2), :]
-        psend[pl.ds(Z // 2 * half, Z // 2)] = block.reshape(Z // 2, SHARE, K).astype(BF16)
+        psend[half, pl.ds(Z // 2 * top, Z // 2)] = (
+            acc[half, pl.ds(OWN // 2 * top, OWN // 2), :]
+            .reshape(Z // 2, SHARE, TS)
+            .astype(BF16)
+        )
+
+    def scatter(phase, half, top):
         for i in range(Z // 2):
-            v = Z // 2 * half + i
+            v = Z // 2 * top + i
 
             @pl.when(z != v)
             def _(v=v):
-                small(4, z, psend.at[v], precv.at[z], z_device(v)).start()
-
-    precv[z] = jnp.zeros((SHARE, K), BF16)
-    result = acc[pl.ds(pl.multiple_of(z * SHARE, SHARE), SHARE), :]
-    recv_z(4, precv)
-    for i in range(Z):
-        result = result + precv[i].astype(F32)
-    embed[...] = result
+                small(phase, z, psend.at[half, v], precv.at[half, z], z_device(v)).start()
+
+    arrange(x)
+    gather_step(5)
+    arrange(mate)
+    early = x // 2
+    products(early, 0)
+    scatter(4, early, 0)
+    gather_step(6)
+    products(early, 1)
+    scatter(4, early, 1)
+    arrange(wrap(x + 2, X))
+    arrange(wrap(mate + 2, X))
+    for top in range(2):
+        products(1 - early, top)
+        scatter(9, 1 - early, top)
+    for half in range(2):
+        precv[half, z] = jnp.zeros((SHARE, TS), BF16)
+    recv_z(4, precv.at[early])
+    recv_z(9, precv.at[1 - early])
+    parts = []
+    for half in range(2):
+        part = acc[half, pl.ds(pl.multiple_of(z * SHARE, SHARE), SHARE), :]
+        for i in range(Z):
+            part = part + precv[half, i].astype(F32)
+        embed[:, pl.ds(TS * half, TS)] = part
+        parts.append(part)
+    result = jnp.concatenate(parts, axis=1)
 
     local_gram = lax.dot_general(
         result,
@@ -403,56 +448,51 @@
         precision=lax.Precision.HIGHEST,
         preferred_element_type=F32,
     ) * (1.0 / NR)
-    left = lax.broadcasted_iota(jnp.int32, (H, TS), 1) < H
-    corner = jnp.where(
-        left, pltpu.roll(local_gram[3 * H :, TS:], H, 1), local_gram[H : 2 * H, :TS]
+    gsrc[...] = (
+        jnp.concatenate([local_gram[:TS, :TS], local_gram[:, TS:]], axis=0)
+        .reshape(U, GROWS, TS)
+        .astype(BF16)
     )
-    gsrc[...] = jnp.concatenate(
-        [local_gram[:H, :TS], local_gram[: 3 * H, TS:], corner], axis=0
-    ).reshape(U, GROWS, TS)
     send_u(5, lambda v: gsrc.at[v], gu)
     gu[u] = gsrc[u]
     recv_u(5, gu)
-    gy[y] = jnp.sum(gu[...], axis=0)
+    gy[y] = total_of(gu).astype(BF16)
     send_y(6, lambda v: gy.at[y], gy)
     recv_y(6, gy)
-    gz[z] = jnp.sum(gy[...], axis=0)
+    gz[z] = total_of(gy).astype(BF16)
     send_z(7, lambda v: gz.at[z], gz)
     recv_z(7, gz)
-    gfin[u] = jnp.sum(gz[...], axis=0)
+    gfin[u] = total_of(gz)
     send_u(8, lambda v: gfin.at[u], gfin)
     recv_u(8, gfin)
-    packed = gfin[...].reshape(5 * H, TS)
-    corner = packed[4 * H :]
-    mirrored = (lax.broadcasted_iota(jnp.int32, (TS, TS), 0) >= H) & (
-        lax.broadcasted_iota(jnp.int32, (TS, TS), 1) < H
-    )
-    first = jnp.concatenate([packed[:H], corner], axis=0)
-    gram[pl.ds(0, TS), pl.ds(0, TS)] = jnp.where(mirrored, first.T, first)
-    across = packed[H : 3 * H]
-    gram[pl.ds(0, TS), pl.ds(TS, TS)] = across
-    gram[pl.ds(TS, TS), pl.ds(0, TS)] = across.T
-    last = jnp.concatenate([packed[3 * H : 4 * H], pltpu.roll(corner, H, 1)], axis=0)
-    gram[pl.ds(TS, TS), pl.ds(TS, TS)] = jnp.where(mirrored, last.T, last)
+    packed = gfin[...].reshape(3 * TS, TS)
+    gram[pl.ds(0, TS), pl.ds(0, TS)] = packed[:TS]
+    gram[:, pl.ds(TS, TS)] = packed[TS:]
+    gram[pl.ds(TS, TS), pl.ds(0, TS)] = packed[TS : 2 * TS].T
 
     sent(0, zrow)
     sent(1, ucol)
     sent(2, ydeg)
     sent(3, udeg)
-    sent(4, precv)
+    sent(4, precv.at[0])
+    sent(9, precv.at[1])
     sent(5, gu)
     sent(6, gy)
     sent(7, gz)
     sent(8, gfin)
-    gone = gath.at[pl.ds(0, ROW - 1)]
-    pltpu.make_async_remote_copy(
-        src_ref=gone,
-        dst_ref=gone,
-        send_sem=ag_send,
-        recv_sem=ag_recv.at[0],
-        device_id=(sibling, z),
-        device_id_type=MESH,
-    ).wait_send()
+    def gone(sem, blocks):
+        view = gath.at[pl.ds(0, blocks)]
+        pltpu.make_async_remote_copy(
+            src_ref=view,
+            dst_ref=view,
+            send_sem=sem,
+            recv_sem=ag_recv.at[0],
+            device_id=(sibling, z),
+            device_id_type=MESH,
+        ).wait_send()
+
+    gone(sib_send, ROW // 2)
+    gone(ag_send, ROW // 2 - 1)
 
 
 def hand_over(embed, gram, embed_out, gram_out):
@@ -468,7 +508,7 @@
         pltpu.VMEM((SLOTS + 1, TS, TS), BF16),
         pltpu.VMEM((ROW, CT * KROWS, TS), BF16),
         pltpu.VMEM((CT, K, TS), BF16),
-        pltpu.VMEM((OWN, K), F32),
+        pltpu.VMEM((2, OWN, TS), F32),
         pltpu.VMEM((KROWS, CT * TS), BF16),
         pltpu.VMEM((8, CT * TS), F32),
         pltpu.VMEM((1, SLOTS), jnp.int32),
@@ -487,20 +527,21 @@
         pltpu.VMEM((U, 16, TS), F32),
         pltpu.VMEM((RT, TS, TS), F32),
         pltpu.VMEM((CT, TS), F32),
-        pltpu.VMEM((Z, SHARE, K), BF16),
-        pltpu.VMEM((Z, SHARE, K), BF16),
-        pltpu.VMEM((U, GROWS, TS), F32),
-        pltpu.VMEM((U, GROWS, TS), F32),
-        pltpu.VMEM((Y, GROWS, TS), F32),
-        pltpu.VMEM((Z, GROWS, TS), F32),
+        pltpu.VMEM((2, Z, SHARE, TS), BF16),
+        pltpu.VMEM((2, Z, SHARE, TS), BF16),
+        pltpu.VMEM((U, GROWS, TS), BF16),
+        pltpu.VMEM((U, GROWS, TS), BF16),
+        pltpu.VMEM((Y, GROWS, TS), BF16),
+        pltpu.VMEM((Z, GROWS, TS), BF16),
         pltpu.VMEM((U, GROWS, TS), F32),
         pltpu.SemaphoreType.DMA((4,)),
         pltpu.SemaphoreType.DMA((6,)),
         pltpu.SemaphoreType.DMA,
         pltpu.SemaphoreType.DMA,
+        pltpu.SemaphoreType.DMA,
         pltpu.SemaphoreType.DMA((ROW,)),
-        pltpu.SemaphoreType.DMA((9,)),
-        pltpu.SemaphoreType.DMA((9, 8)),
+        pltpu.SemaphoreType.DMA((10,)),
+        pltpu.SemaphoreType.DMA((10, 8)),
     ]
     embed, gram = pl.pallas_call(
         kernel,

time: 80.2 us -> 78.4 us (0.978)
  Pallas kernels: 78.8 us -> 77 us
    pallas_call x1, Pallas kernels: 77.1 us -> 75.2 us  [local(): pl.pallas_call(kernel, out_shape=(jax.ShapeDtypeStruct((SHARE, K), F32),...]
where the time goes in v3:
time: 78.4 us; the launch traced here: 78.2 us
  Pallas kernels  77 us (98%)
  between operations  1.28 us (2%)
    pallas_call x1, Pallas kernels, local(): pl.pallas_call(kernel, out_shape=(jax.ShapeDtypeStruct((SHARE, K), F32),...  75.2 us
    pallas_call x1, Pallas kernels, local(): pl.pallas_call(hand_over, out_shape=(jax.ShapeDtypeStruct((SHARE, K), F32...  1.72 us

profile of v3, /device:TPU:1, one launch (start us, length us, event | category | flops | bytes accessed | tf_op | source)
XLA Modules:
  0.0 78.2 jit_solution(3356192727924544138)
XLA Ops:
  1.3 75.2 %shard_map.68 = (f32[64,256]{1,0:T(8,128)}, f32[256,256]{1,0:T(8,128)}) custom-call(s32[1,128]{1,0:T(1,128)} %bitcast.2, s32[1,128]{1,0:T(1,128)} %bitcast.3, s32[1]{0:T(128)S(6)} %copy.7.count_h, bf16[4,8192]{1,0:T(4,128)(2,1)} %sketch_h.1, bf16[128,128,128]{2,1,0:T(8,128)(2,1)} %tiles.1), custom_call_target="tpu_custom_call" | custom-call | tf_op jit(solution)/shard_map/pallas_call | solution.py:546
  76.5 1.7 %shard_map.69 = (f32[64,256]{1,0:T(8,128)}, f32[256,256]{1,0:T(8,128)}) custom-call(f32[64,256]{1,0:T(8,128)} %get-tuple-element.4.embed, f32[256,256]{1,0:T(8,128)} %get-tuple-element.5.gram), custom_call_target="tpu_custom_call" | custom-call | tf_op jit(solution)/shard_map/pallas_call | solution.py:565

commit v4 on v3

--- a/solution.py
+++ b/solution.py
@@ -254,23 +254,36 @@
         along_x(d)
         to_sibling(d)
 
-    def near(m):
-        yy = y_peer(m)
-        sign = 1 - 2 * lax.rem(yy, 2)
-        relayed = rid(wrap(x - sign, X), yy)
-        other = rid(wrap(x + sign, X), yy)
-        arrived(relayed)
-        block_copy(relayed, rid(wrap(x + sign, X), y)).start()
-        to_sibling(relayed)
-        arrived(other)
-        to_sibling(other)
+    def x_pair(m):
+        sign = 1 if m in (0, 1, 2, 3) else -1
+        return sign, y_peer(m)
+
+    def relay(m):
+        sign, yy = x_pair(m)
+        d = rid(wrap(x - sign, X), yy)
+        arrived(d)
+        block_copy(d, rid(wrap(x + sign, X), y)).start()
+        to_sibling(d)
+
+    def other(m):
+        sign, yy = x_pair(m)
+        d = rid(wrap(x + sign, X), yy)
+        arrived(d)
+        to_sibling(d)
 
     def far(m):
         d = rid(wrap(x + 2, X), y_peer(m))
         arrived(d)
         to_sibling(d)
 
-    rings = ((0,), (1, -1), (2, -2), (3, -3), (4,))
+    steps = (
+        ((by_y, (1, -1)), (relay, (0,))),
+        ((by_y, (2, -2)), (relay, (1, -1)), (other, (0,))),
+        ((by_y, (3, -3, 4)), (relay, (2, -2)), (other, (1, -1))),
+        ((relay, (3, -3, 4)), (other, (2, -2)), (far, (0, 1, -1))),
+        ((other, (3, -3, 4)), (far, (2, -2))),
+        ((far, (3, -3, 4)),),
+    )
 
     def gather_step(t):
         if t == 0:
@@ -278,12 +291,9 @@
             along_y(row, 0)
             to_sibling(row)
             return
-        for f, i in ((by_y, t), (near, t - 1), (far, t - 2)):
-            if 0 <= i < len(rings):
-                for m in rings[i]:
-                    if f is not by_y or m != 0:
-                        f(m)
-
+        for f, ms in steps[t - 1]:
+            for m in ms:
+                f(m)
 
     def small(phase, slot, src, dst, device):
         return pltpu.make_async_remote_copy(

time: 78.4 us -> 75.1 us (0.958)
  Pallas kernels: 77 us -> 73.6 us
    pallas_call x1, Pallas kernels: 75.2 us -> 71.9 us  [local(): pl.pallas_call(kernel, out_shape=(jax.ShapeDtypeStruct((SHARE, K), F32),...]
where the time goes in v4:
time: 75.1 us; the launch traced here: 74.9 us
  Pallas kernels  73.6 us (98%)
  between operations  1.28 us (2%)
    pallas_call x1, Pallas kernels, local(): pl.pallas_call(kernel, out_shape=(jax.ShapeDtypeStruct((SHARE, K), F32),...  71.9 us
    pallas_call x1, Pallas kernels, local(): pl.pallas_call(hand_over, out_shape=(jax.ShapeDtypeStruct((SHARE, K), F32...  1.72 us

profile of v4, /device:TPU:1, one launch (start us, length us, event | category | flops | bytes accessed | tf_op | source)
XLA Modules:
  0.0 74.9 jit_solution(16889488849657650695)
XLA Ops:
  1.3 71.9 %shard_map.68 = (f32[64,256]{1,0:T(8,128)}, f32[256,256]{1,0:T(8,128)}) custom-call(s32[1,128]{1,0:T(1,128)} %bitcast.2, s32[1,128]{1,0:T(1,128)} %bitcast.3, s32[1]{0:T(128)S(6)} %copy.7.count_h, bf16[4,8192]{1,0:T(4,128)(2,1)} %sketch_h.1, bf16[128,128,128]{2,1,0:T(8,128)(2,1)} %tiles.1), custom_call_target="tpu_custom_call" | custom-call | tf_op jit(solution)/shard_map/pallas_call | solution.py:556
  73.2 1.7 %shard_map.69 = (f32[64,256]{1,0:T(8,128)}, f32[256,256]{1,0:T(8,128)}) custom-call(f32[64,256]{1,0:T(8,128)} %get-tuple-element.4.embed, f32[256,256]{1,0:T(8,128)} %get-tuple-element.5.gram), custom_call_target="tpu_custom_call" | custom-call | tf_op jit(solution)/shard_map/pallas_call | solution.py:575

commit v5 on v4

--- a/solution.py
+++ b/solution.py
@@ -51,7 +51,7 @@
     sketch_h,
     tiles,
     embed,
-    gram,
+    blocks,
     a,
     logm,
     gath,
@@ -475,10 +475,7 @@
     gfin[u] = total_of(gz)
     send_u(8, lambda v: gfin.at[u], gfin)
     recv_u(8, gfin)
-    packed = gfin[...].reshape(3 * TS, TS)
-    gram[pl.ds(0, TS), pl.ds(0, TS)] = packed[:TS]
-    gram[:, pl.ds(TS, TS)] = packed[TS:]
-    gram[pl.ds(TS, TS), pl.ds(0, TS)] = packed[TS : 2 * TS].T
+    blocks[...] = gfin[...].reshape(3 * TS, TS)
 
     sent(0, zrow)
     sent(1, ucol)
@@ -505,9 +502,11 @@
     gone(ag_send, ROW // 2 - 1)
 
 
-def hand_over(embed, gram, embed_out, gram_out):
+def hand_over(embed, blocks, embed_out, gram_out):
     embed_out[...] = embed[...]
-    gram_out[...] = gram[...]
+    gram_out[pl.ds(0, TS), pl.ds(0, TS)] = blocks[pl.ds(0, TS), :]
+    gram_out[:, pl.ds(TS, TS)] = blocks[pl.ds(TS, 2 * TS), :]
+    gram_out[pl.ds(TS, TS), pl.ds(0, TS)] = blocks[pl.ds(TS, TS), :].T
 
 
 def local(tile_values, tile_rows, tile_cols, tile_count, sketch):
@@ -553,11 +552,11 @@
         pltpu.SemaphoreType.DMA((10,)),
         pltpu.SemaphoreType.DMA((10, 8)),
     ]
-    embed, gram = pl.pallas_call(
+    embed, blocks = pl.pallas_call(
         kernel,
         out_shape=(
             jax.ShapeDtypeStruct((SHARE, K), F32),
-            jax.ShapeDtypeStruct((K, K), F32),
+            jax.ShapeDtypeStruct((3 * TS, TS), F32),
         ),
         in_specs=[hbm] * 5,
         out_specs=(vmem, vmem),
@@ -580,7 +579,7 @@
         ),
         in_specs=[vmem] * 2,
         out_specs=(vmem, vmem),
-    )(embed, gram)
+    )(embed, blocks)
 
 
 def solution(mesh):

time: 75.1 us -> 75 us (level)
  no operation moved by 1% of the time
where the time goes in v5:
time: 75 us; the launch traced here: 74.9 us
  Pallas kernels  73.6 us (98%)
  between operations  1.28 us (2%)
    pallas_call x1, Pallas kernels, local(): pl.pallas_call(kernel, out_shape=(jax.ShapeDtypeStruct((SHARE, K), F32),...  71.8 us
    pallas_call x1, Pallas kernels, local(): pl.pallas_call(hand_over, out_shape=(jax.ShapeDtypeStruct((SHARE, K), F32...  1.77 us

profile of v5, /device:TPU:1, one launch (start us, length us, event | category | flops | bytes accessed | tf_op | source)
XLA Modules:
  0.0 74.9 jit_solution(12138402287004783634)
XLA Ops:
  1.3 71.8 %shard_map.68 = (f32[64,256]{1,0:T(8,128)}, f32[384,128]{1,0:T(8,128)}) custom-call(s32[1,128]{1,0:T(1,128)} %bitcast.2, s32[1,128]{1,0:T(1,128)} %bitcast.3, s32[1]{0:T(128)S(6)} %copy.7.count_h, bf16[4,8192]{1,0:T(4,128)(2,1)} %sketch_h.1, bf16[128,128,128]{2,1,0:T(8,128)(2,1)} %tiles.1), custom_call_target="tpu_custom_call" | custom-call | tf_op jit(solution)/shard_map/pallas_call | solution.py:555
  73.1 1.8 %shard_map.69 = (f32[64,256]{1,0:T(8,128)}, f32[256,256]{1,0:T(8,128)}) custom-call(f32[64,256]{1,0:T(8,128)} %get-tuple-element.4.embed, f32[384,128]{1,0:T(8,128)} %get-tuple-element.5.blocks), custom_call_target="tpu_custom_call" | custom-call | tf_op jit(solution)/shard_map/pallas_call | solution.py:574
